TPU v7x, 128 devices: a whole 4x4x4 slice. The times are simulated.
128 devices in a mesh: patch: 8 (over z, x_lo), head: 16 (over x_hi, y, core).
Axes of the slice: x: 4 (x_hi: 2, x_lo: 2; x = x_hi * 2 + x_lo), y: 4, z: 4, core: 2. Of those that a mesh axis runs over, the one named last changes fastest.
Arguments:
- fresh_qkv: bfloat16 [16384, 3, 2048], P(('patch', 'head')), may hold values from -20 to 20
- stale_kv: bfloat16 [16384, 2, 2048], P(('patch', 'head')), may hold values from -20 to 20
- out_weight: bfloat16 [2048, 3072], replicated, may hold values from -0.375 to 0.375
Outputs:
- mixed: bfloat16 [16384, 3072], P(('patch', 'head'))
All inputs are finite; a program needn't handle non-finite values.
Results may differ from a plain program's by a relative error of at most 0.0095.
Values may be sent and summed in bfloat16 or wider, within the bound.
A program may use at most 128 MiB of HBM per device.

v0:
```python
import jax
import jax.numpy as jnp
from jax import lax
from jax.sharding import PartitionSpec as P

HEAD_DIM = 128


def block_scores(query_block, keys):
    return jnp.einsum(
        "qhd,khd->hqk", query_block, keys, preferred_element_type=jnp.float32
    ) * keys.shape[2] ** (-0.5)


def on_device(fresh_qkv, stale_kv, out_weight):
    fresh_local, stale_local = (
        lax.all_to_all(fresh_qkv, "head", split_axis=2, concat_axis=0, tiled=True),
        lax.all_to_all(stale_kv, "head", split_axis=2, concat_axis=0, tiled=True),
    )
    patch_rows = fresh_local.shape[0]
    width = fresh_local.shape[2]
    head_dim = HEAD_DIM
    local_heads = width // head_dim
    block = min(512, patch_rows)
    blocks = patch_rows // block
    my_start = lax.axis_index("patch") * patch_rows
    queries = fresh_local[:, 0, :].reshape(blocks, block, local_heads, head_dim)
    gathered = lax.all_gather(stale_local, "patch", axis=0, tiled=True)
    merged = lax.dynamic_update_slice_in_dim(gathered, fresh_local[:, 1:3, :], my_start, 0)
    rows_all = merged.shape[0]
    keys = merged[:, 0, :].reshape(rows_all, local_heads, head_dim)
    values = merged[:, 1, :].reshape(rows_all, local_heads, head_dim)

    def one_block(query_block):
        scores = block_scores(query_block, keys)
        peak = jnp.max(scores, axis=2, keepdims=True)
        expo = jnp.exp(scores - peak)
        total = jnp.sum(expo, axis=2)
        summed = jnp.einsum(
            "hqk,khd->qhd", expo.astype(jnp.bfloat16), values, preferred_element_type=jnp.float32
        )
        return summed / total.T[:, :, None]

    attended = lax.map(one_block, queries)
    attended = attended.reshape(patch_rows, width).astype(jnp.bfloat16)
    token_rows = lax.all_to_all(attended, "head", split_axis=0, concat_axis=1, tiled=True)
    return jnp.dot(token_rows, out_weight, preferred_element_type=jnp.float32).astype(jnp.bfloat16)


def solution(mesh):
    return jax.shard_map(
        on_device,
        mesh=mesh,
        in_specs=(P(("patch", "head"), None, None), P(("patch", "head"), None, None), P()),
        out_specs=P(("patch", "head"), None),
        check_vma=False,
    )
```

profile of v0, /device:TPU:1, one launch (start us, length us, event | category | flops | bytes accessed | tf_op | source)
XLA Modules:
  0.0 443.1 jit_solution(5584702513840764205)
XLA Ops:
  6.5 0.0 all-gather.2.cloned.1.call-start
  6.5 4.6 %copy.20 = bf16[128,2,2048]{0,1,2:T(2,128)(2,1)S(1)} copy(bf16[128,2,2048]{2,1,0:T(2,128)(2,1)} %param.6) | data formatting | bytes 2097152 | tf_op args[1]
  11.1 25.2 %all_to_all.52 = bf16[128,2,2048]{0,1,2:T(2,128)(2,1)S(1)} all-to-all(bf16[128,2,2048]{0,1,2:T(2,128)(2,1)S(1)} %copy.20), channel_id=1, replica_groups=mesh['patch'=8,'head'=16] {'head'}, dimensions={2} | all-to-all | bytes 2097152 | tf_op jit(solution)/shard_map/all_to_all | solution.py:18
  36.3 2.0 copy.21
  38.3 0.0 all-gather.2.cloned.1.call-update
  38.3 4.2 copy.18
  42.5 4.7 %all-to-all-start = ((bf16[128,3,2048]{0,1,2:T(4,128)(2,1)}), bf16[128,3,2048]{0,1,2:T(4,128)(2,1)S(1)}, u32[]{:S(2)}, u32[]{:S(2)}) async-start(bf16[128,3,2048]{0,1,2:T(4,128)(2,1)} %copy.18), calls=%async_computation | async-start | bytes 4194304 | tf_op jit(solution)/shard_map/all_to_all | solution.py:17
  47.2 51.3 %all-to-all-done = bf16[128,3,2048]{0,1,2:T(4,128)(2,1)S(1)} async-done(((bf16[128,3,2048]{0,1,2:T(4,128)(2,1)}), bf16[128,3,2048]{0,1,2:T(4,128)(2,1)S(1)}, u32[]{:S(2)}, u32[]{:S(2)}) %all-to-all-start) | async-done | bytes 1572896 | tf_op jit(solution)/shard_map/all_to_all | solution.py:17
  98.4 2.4 copy.19
  100.8 1.1 slice.16
  101.9 126.0 %all-gather.2.cloned.1.call-done = bf16[16384,2,128]{2,0,1:T(8,128)(2,1)} async-done(((bf16[2048,2,128]{2,0,1:T(8,128)(2,1)}), bf16[16384,2,128]{2,0,1:T(8,128)(2,1)}) %all-gather.2.cloned.1.call-update) | async-done | bytes 8388624 | tf_op jit(solution)/shard_map/all_gather | solution.py:28
  227.9 2.4 slice_dynamic-update-slice_fusion
  230.3 5.7 %fusion.31 = (bf16[16384,1,128]{2,0,1:T(8,128)(2,1)}, bf16[16384,1,128]{2,0,1:T(8,128)(2,1)}) fusion(bf16[16384,2,128]{2,0,1:T(8,128)(2,1)} %slice_dynamic-update-slice_fusion), kind=kLoop, calls=%fused_computation.19 | loop fusion | bytes 16777216 | tf_op jit(solution)/shard_map/slice | solution.py:32
  235.9 174.5 %while.10 = (s32[]{:T(128)}, bf16[4,512,1,128]{3,1,2,0:T(8,128)(2,1)S(1)}, bf16[4,512,1,128]{3,1,2,0:T(8,128)(2,1)S(1)}, bf16[16384,1,128]{2,0,1:T(8,128)(2,1)}, bf16[16384,1,128]{2,0,1:T(8,128)(2,1)}, /*index=5*/s32[]{:T(128)}) while((s32[]{:T(128)}, bf16[4,512,1,128]{3,1,2,0:T(8,128)(2,1)S(1)}, bf16[4,512,1,128]{3,1,2,0:T(8,128)(2,1)S(1)}, ...), condition=%wide.region_3.4_spmd, body=%wide.region_0.3_spmd.sunk | while | flops 4362140672 | bytes 126232680 | solution.py:44
  235.9 15.2 %multiply_reduce_fusion.2 = (f32[512]{0:T(512)S(1)}, f32[512,16384]{1,0:T(8,128)}) fusion(bf16[16384,1,128]{2,0,1:T(8,128)(2,1)} %get-tuple-element.97, bf16[4,512,1,128]{3,1,2,0:T(8,128)(2,1)S(1)} %get-tuple-element.96, s32[]{:T(128)} %get-tuple-element.88), kind=kOutput, calls=%fused_computation.1.clone.1 | convolution fusion | flops 2164260352 | bytes 37881860 | tf_op jit(solution)/shard_map/while/body/eval_jaxpr/qhd,khd->hqk/dot_general | solution.py:10
  251.2 0.0 copy-start
  251.2 14.3 %fusion.40 = f32[512]{0:T(512)S(1)} fusion(f32[512,16384]{1,0:T(8,128)} %get-tuple-element.80, f32[512]{0:T(512)S(1)} %get-tuple-element.81), kind=kLoop, calls=%fused_computation.2.clone.1 | loop fusion | flops 25165312 | bytes 33558528 | tf_op jit(solution)/shard_map/while/body/eval_jaxpr/reduce_sum | solution.py:38
  265.5 0.0 copy-done
  265.5 14.1 %fusion.41 = bf16[4,512,1,128]{3,1,2,0:T(8,128)(2,1)S(1)} fusion(bf16[4,512,1,128]{3,1,2,0:T(8,128)(2,1)S(1)} %get-tuple-element.89, s32[]{:T(128)} %get-tuple-element.88, bf16[16384,1,128]{2,0,1:T(8,128)(2,1)S(1)} %copy-done, f32[512,16384]{1,0:T(8,128)} %get-tuple-element.80, f32[512]{0:T(512)S(1)} %get-tuple-element.81, f32[512]{0:T(512)S(1)} %fusion.40), kind=kOutput, calls=%fused_computation.11.clone.1 | convolution fusion | flops 2172715008 | bytes 38014980 | tf_op jit(solution)/shard_map/while/body/eval_jaxpr/hqk,khd->qhd/dot_general | solution.py:39
  279.6 15.3 %multiply_reduce_fusion.2 = (f32[512]{0:T(512)S(1)}, f32[512,16384]{1,0:T(8,128)}) fusion(bf16[16384,1,128]{2,0,1:T(8,128)(2,1)} %get-tuple-element.97, bf16[4,512,1,128]{3,1,2,0:T(8,128)(2,1)S(1)} %get-tuple-element.96, s32[]{:T(128)} %get-tuple-element.88), kind=kOutput, calls=%fused_computation.1.clone.1 | convolution fusion | flops 2164260352 | bytes 37881860 | tf_op jit(solution)/shard_map/while/body/eval_jaxpr/qhd,khd->hqk/dot_general | solution.py:10
  294.8 0.0 copy-start
  294.8 14.3 %fusion.40 = f32[512]{0:T(512)S(1)} fusion(f32[512,16384]{1,0:T(8,128)} %get-tuple-element.80, f32[512]{0:T(512)S(1)} %get-tuple-element.81), kind=kLoop, calls=%fused_computation.2.clone.1 | loop fusion | flops 25165312 | bytes 33558528 | tf_op jit(solution)/shard_map/while/body/eval_jaxpr/reduce_sum | solution.py:38
  309.1 0.0 copy-done
  309.1 14.1 %fusion.41 = bf16[4,512,1,128]{3,1,2,0:T(8,128)(2,1)S(1)} fusion(bf16[4,512,1,128]{3,1,2,0:T(8,128)(2,1)S(1)} %get-tuple-element.89, s32[]{:T(128)} %get-tuple-element.88, bf16[16384,1,128]{2,0,1:T(8,128)(2,1)S(1)} %copy-done, f32[512,16384]{1,0:T(8,128)} %get-tuple-element.80, f32[512]{0:T(512)S(1)} %get-tuple-element.81, f32[512]{0:T(512)S(1)} %fusion.40), kind=kOutput, calls=%fused_computation.11.clone.1 | convolution fusion | flops 2172715008 | bytes 38014980 | tf_op jit(solution)/shard_map/while/body/eval_jaxpr/hqk,khd->qhd/dot_general | solution.py:39
  323.2 15.3 %multiply_reduce_fusion.2 = (f32[512]{0:T(512)S(1)}, f32[512,16384]{1,0:T(8,128)}) fusion(bf16[16384,1,128]{2,0,1:T(8,128)(2,1)} %get-tuple-element.97, bf16[4,512,1,128]{3,1,2,0:T(8,128)(2,1)S(1)} %get-tuple-element.96, s32[]{:T(128)} %get-tuple-element.88), kind=kOutput, calls=%fused_computation.1.clone.1 | convolution fusion | flops 2164260352 | bytes 37881860 | tf_op jit(solution)/shard_map/while/body/eval_jaxpr/qhd,khd->hqk/dot_general | solution.py:10
  338.5 0.0 copy-start
  338.5 14.3 %fusion.40 = f32[512]{0:T(512)S(1)} fusion(f32[512,16384]{1,0:T(8,128)} %get-tuple-element.80, f32[512]{0:T(512)S(1)} %get-tuple-element.81), kind=kLoop, calls=%fused_computation.2.clone.1 | loop fusion | flops 25165312 | bytes 33558528 | tf_op jit(solution)/shard_map/while/body/eval_jaxpr/reduce_sum | solution.py:38
  352.8 0.0 copy-done
  352.8 14.1 %fusion.41 = bf16[4,512,1,128]{3,1,2,0:T(8,128)(2,1)S(1)} fusion(bf16[4,512,1,128]{3,1,2,0:T(8,128)(2,1)S(1)} %get-tuple-element.89, s32[]{:T(128)} %get-tuple-element.88, bf16[16384,1,128]{2,0,1:T(8,128)(2,1)S(1)} %copy-done, f32[512,16384]{1,0:T(8,128)} %get-tuple-element.80, f32[512]{0:T(512)S(1)} %get-tuple-element.81, f32[512]{0:T(512)S(1)} %fusion.40), kind=kOutput, calls=%fused_computation.11.clone.1 | convolution fusion | flops 2172715008 | bytes 38014980 | tf_op jit(solution)/shard_map/while/body/eval_jaxpr/hqk,khd->qhd/dot_general | solution.py:39
  366.9 15.3 %multiply_reduce_fusion.2 = (f32[512]{0:T(512)S(1)}, f32[512,16384]{1,0:T(8,128)}) fusion(bf16[16384,1,128]{2,0,1:T(8,128)(2,1)} %get-tuple-element.97, bf16[4,512,1,128]{3,1,2,0:T(8,128)(2,1)S(1)} %get-tuple-element.96, s32[]{:T(128)} %get-tuple-element.88), kind=kOutput, calls=%fused_computation.1.clone.1 | convolution fusion | flops 2164260352 | bytes 37881860 | tf_op jit(solution)/shard_map/while/body/eval_jaxpr/qhd,khd->hqk/dot_general | solution.py:10
  382.1 0.0 copy-start
  382.1 14.3 %fusion.40 = f32[512]{0:T(512)S(1)} fusion(f32[512,16384]{1,0:T(8,128)} %get-tuple-element.80, f32[512]{0:T(512)S(1)} %get-tuple-element.81), kind=kLoop, calls=%fused_computation.2.clone.1 | loop fusion | flops 25165312 | bytes 33558528 | tf_op jit(solution)/shard_map/while/body/eval_jaxpr/reduce_sum | solution.py:38
  396.4 0.0 copy-done
  396.4 14.1 %fusion.41 = bf16[4,512,1,128]{3,1,2,0:T(8,128)(2,1)S(1)} fusion(bf16[4,512,1,128]{3,1,2,0:T(8,128)(2,1)S(1)} %get-tuple-element.89, s32[]{:T(128)} %get-tuple-element.88, bf16[16384,1,128]{2,0,1:T(8,128)(2,1)S(1)} %copy-done, f32[512,16384]{1,0:T(8,128)} %get-tuple-element.80, f32[512]{0:T(512)S(1)} %get-tuple-element.81, f32[512]{0:T(512)S(1)} %fusion.40), kind=kOutput, calls=%fused_computation.11.clone.1 | convolution fusion | flops 2172715008 | bytes 38014980 | tf_op jit(solution)/shard_map/while/body/eval_jaxpr/hqk,khd->qhd/dot_general | solution.py:39
  410.5 18.2 %all_to_all.53 = bf16[16,128,128]{2,1,0:T(8,128)(2,1)S(1)} all-to-all(bf16[16,128,128]{2,1,0:T(8,128)(2,1)S(1)} %bitcast.72), channel_id=1, replica_groups=mesh['patch'=8,'head'=16] {'head'}, dimensions={0} | all-to-all | bytes 1048576 | tf_op jit(solution)/shard_map/all_to_all | solution.py:46
  428.7 0.3 copy.23
  429.0 7.3 %convolution_convert_fusion = bf16[128,3072]{1,0:T(8,128)(2,1)} fusion(bf16[128,2048]{0,1:T(8,128)(2,1)S(1)} %bitcast.69, bf16[2048,3072]{1,0:T(8,128)(2,1)} %param.7), kind=kOutput, calls=%fused_computation.16 | convolution fusion | flops 1611005952 | bytes 13893632 | tf_op jit(solution)/shard_map/dot_general | solution.py:47
  (1 shorter events, 0.0 us)
Async XLA Ops:
  6.5 221.4 %all-gather.2.cloned.1.call-start = ((), (), s32[]{:S(2)}) async-start(), calls=%async_computation.3 | async-start | bytes 9437184 | tf_op jit(solution)/shard_map/all_gather | solution.py:28
  42.5 55.9 %all-to-all-start = ((bf16[128,3,2048]{0,1,2:T(4,128)(2,1)}), bf16[128,3,2048]{0,1,2:T(4,128)(2,1)S(1)}, u32[]{:S(2)}, u32[]{:S(2)}) async-start(bf16[128,3,2048]{0,1,2:T(4,128)(2,1)} %copy.18), calls=%async_computation | async-start | bytes 4194304 | tf_op jit(solution)/shard_map/all_to_all | solution.py:17
  251.2 14.3 %copy-start = (bf16[16384,1,128]{2,0,1:T(8,128)(2,1)S(1)}, bf16[16384,1,128]{2,0,1:T(8,128)(2,1)}, u32[]{:S(2)}) copy-start(bf16[16384,1,128]{2,0,1:T(8,128)(2,1)} %get-tuple-element.98) | copy-start | bytes 12582916 | tf_op jit(solution)/shard_map/while
  294.8 14.3 %copy-start = (bf16[16384,1,128]{2,0,1:T(8,128)(2,1)S(1)}, bf16[16384,1,128]{2,0,1:T(8,128)(2,1)}, u32[]{:S(2)}) copy-start(bf16[16384,1,128]{2,0,1:T(8,128)(2,1)} %get-tuple-element.98) | copy-start | bytes 12582916 | tf_op jit(solution)/shard_map/while
  338.5 14.3 %copy-start = (bf16[16384,1,128]{2,0,1:T(8,128)(2,1)S(1)}, bf16[16384,1,128]{2,0,1:T(8,128)(2,1)}, u32[]{:S(2)}) copy-start(bf16[16384,1,128]{2,0,1:T(8,128)(2,1)} %get-tuple-element.98) | copy-start | bytes 12582916 | tf_op jit(solution)/shard_map/while
  382.1 14.3 %copy-start = (bf16[16384,1,128]{2,0,1:T(8,128)(2,1)S(1)}, bf16[16384,1,128]{2,0,1:T(8,128)(2,1)}, u32[]{:S(2)}) copy-start(bf16[16384,1,128]{2,0,1:T(8,128)(2,1)} %get-tuple-element.98) | copy-start | bytes 12582916 | tf_op jit(solution)/shard_map/while
Sparse Core Ops, SparseCore 0:
  38.4 189.3 all-gather.1
where the time goes:
time: 444 us; the launch traced here: 443 us
  waiting for transfers between devices  177 us (40%)
  matrix products  125 us (28%)
  other arithmetic  57.1 us (13%)
  blocking collectives  43.3 us (10%)
  local copies, waits for them, and re-layouts  22.6 us (5%)
  between operations  13.4 us (3%)
  starting transfers between devices  4.67 us (1%)
    all_gather x1, waiting for transfers between devices, on_device(): gathered = lax.all_gather(stale_local, 'patch', axis=0, tiled=True)  126 us
    dot_general x4, matrix products, block_scores(): jnp.einsum('qhd,khd->hqk', query_block, keys, preferred_element_type=jnp....  61 us
    reduce_sum x4, other arithmetic, one_block(): total = jnp.sum(expo, axis=2)  57.1 us
    dot_general x4, matrix products, one_block(): jnp.einsum('hqk,khd->qhd', expo.astype(jnp.bfloat16), values, preferred_e...  56.2 us
    all_to_all x1, waiting for transfers between devices, on_device(): lax.all_to_all(fresh_qkv, 'head', split_axis=2, concat_axis=0, tiled=True)  51.3 us
    all_to_all x1, blocking collectives, on_device(): lax.all_to_all(stale_kv, 'head', split_axis=2, concat_axis=0, tiled=True)  25.2 us
    all_to_all x1, blocking collectives, on_device(): lax.all_to_all(attended, 'head', split_axis=0, concat_axis=1, tiled=True)  18.2 us
  transfers between devices with their start and end apart: 2, of which 2 were waited for; matrix products, arithmetic and copies ran while one was open for 2% of the time, Pallas kernels for 0%

commit v1 on v0

v1 whole, which is shorter than its diff:
```python
import jax
import jax.numpy as jnp
from jax import lax
from jax.experimental import pallas as pl
from jax.experimental.pallas import tpu as pltpu
from jax.sharding import PartitionSpec as P

MESH = pl.DeviceIdType.MESH
BLK = 128
STEP = 512
QB = 1024
FACTOR = float(128 ** -0.5 * 1.4426950408889634)
F32 = jnp.float32
BF16 = jnp.bfloat16


def kernel(fresh, stale, weight, out,
           wbuf, send_s, send_f, kv, qbuf, acc_s, m_s, l_s, sbuf, po, pml, po_in, pml_in, a_out, a_in,
           w_sem, q_send, q_recv, qx_send, qx_recv, s_send, s_recv, f_send, f_recv,
           up_send, up_recv, dn_send, dn_recv, up2_send, up2_recv, dn2_send, dn2_recv,
           po_send, po_recv, pml_send, pml_recv, a_send, a_recv, own_sem):
    p, hd = lax.axis_index("patch"), lax.axis_index("head")
    z, xl = p // 2, p % 2
    xh, j = hd // 8, hd % 8
    me = xl * 8 + j
    my_head = (xl + xh - 2 * xl * xh) * 8 + j
    above = (2 * ((z + 1) % 4) + xl, hd)
    below = (2 * ((z + 3) % 4) + xl, hd)
    partner = (2 * z + 1 - xl, (1 - xh) * 8 + j)

    def member(t):
        tl, tj = t // 8, t % 8
        return (2 * z + tl, xh * 8 + tj), (tl + xh - 2 * tl * xh) * 8 + tj

    def remote(src, dst, send, recv, to):
        return pltpu.make_async_remote_copy(
            src_ref=src, dst_ref=dst, send_sem=send, recv_sem=recv, device_id=to, device_id_type=MESH)

    def wait_bytes(ref, sem):
        pltpu.make_async_copy(ref, ref, sem).wait()

    barrier = pltpu.get_barrier_semaphore()

    def greet(d, c):
        to, _ = member((me + d) % 16)
        pl.semaphore_signal(barrier, inc=1, device_id=to, device_id_type=MESH)
        return c

    lax.fori_loop(1, 16, greet, 0)
    for to in (above, below, partner):
        pl.semaphore_signal(barrier, inc=1, device_id=to, device_id_type=MESH)

    weight_copy = pltpu.make_async_copy(weight, wbuf, w_sem)

    def pack(source, k_row, buf):
        for h in range(16):
            cols = slice(h * BLK, (h + 1) * BLK)
            buf[h, 0] = source[k_row, :, cols]
            buf[h, 1] = source[k_row + 1, :, cols].T

    pack(stale, 0, send_s)
    pl.semaphore_wait(barrier, 18)

    def lane(h):
        return pl.ds(pl.multiple_of(h * BLK, BLK), BLK)

    def send_q(d, c):
        to, h = member((me + d) % 16)
        remote(fresh.at[0, :, lane(h)], qbuf.at[0, xl, j], q_send, q_recv, to).start()
        return c

    lax.fori_loop(1, 16, send_q, 0)
    pltpu.make_async_copy(fresh.at[0, :, lane(my_head)], qbuf.at[0, xl, j], q_recv).start()

    def send_stale(d, c):
        to, h = member((me + d) % 16)
        remote(send_s.at[h], kv.at[2 * z + xl, j], s_send, s_recv.at[me], to).start()
        return c

    lax.fori_loop(1, 16, send_stale, 0)
    pltpu.make_async_copy(send_s.at[my_head], kv.at[2 * z + xl, j], s_recv.at[me]).start()

    pack(fresh, 1, send_f)

    def send_fresh(d, c):
        to, h = member((me + d) % 16)
        remote(send_f.at[h], kv.at[8 + xl, j], f_send, f_recv, to).start()
        return c

    lax.fori_loop(1, 16, send_fresh, 0)
    pltpu.make_async_copy(send_f.at[my_head], kv.at[8 + xl, j], f_recv).start()
    weight_copy.start()

    wait_bytes(qbuf.at[0], q_recv)
    qx = remote(qbuf.at[0], qbuf.at[1], qx_send, qx_recv, partner)
    qx.start()

    def forward(i, c):
        t = (me + 16 - i) % 16
        slot = kv.at[2 * z + t // 8, t % 8]
        wait_bytes(slot, s_recv.at[t])
        remote(slot, slot, up_send, up_recv.at[t], above).start()
        remote(slot, slot, dn_send, dn_recv.at[t], below).start()
        return c

    lax.fori_loop(0, 16, forward, 0)

    def scores(qb, slab, half):
        keys = kv[slab, half * 4:half * 4 + 4, 0].reshape(STEP, BLK)
        queries = qbuf[qb // 2, qb % 2].reshape(QB, BLK)
        return lax.dot_general(keys, queries, (((1,), (1,)), ((), ())), preferred_element_type=F32)

    def weighted(slab, half, weights):
        values = jnp.concatenate([kv[slab, half * 4 + c, 1] for c in range(4)], axis=1)
        return jnp.dot(values, weights, preferred_element_type=F32)

    def phase(order, count, slabs, first, finish):
        steps = [(slab, half) for slab in slabs for half in range(2)]
        sbuf[...] = scores(order(0), steps[0][0](order(0)), steps[0][1])

        def block(i, c):
            qb = order(i)
            following = order(jnp.minimum(i + 1, count - 1))
            if not first:
                m, l, acc = m_s[qb, 0:1], l_s[qb, 0:1], acc_s[qb]
            s = sbuf[...]
            for n, (slab, half) in enumerate(steps):
                if n + 1 < len(steps):
                    upcoming = scores(qb, steps[n + 1][0](qb), steps[n + 1][1])
                else:
                    sbuf[...] = scores(following, steps[0][0](following), steps[0][1])
                peak = jnp.max(s, axis=0, keepdims=True) * FACTOR
                if first and n == 0:
                    m = peak
                    w = jnp.exp2(s * FACTOR - m)
                    l = jnp.sum(w, axis=0, keepdims=True)
                    acc = weighted(slab(qb), half, w.astype(BF16))
                else:
                    new = jnp.maximum(m, peak)
                    shrink = jnp.exp2(m - new)
                    m = new
                    w = jnp.exp2(s * FACTOR - m)
                    l = l * shrink + jnp.sum(w, axis=0, keepdims=True)
                    acc = acc * shrink + weighted(slab(qb), half, w.astype(BF16))
                s = upcoming
            if finish is None:
                m_s[qb, 0:1], l_s[qb, 0:1], acc_s[qb] = m, l, acc
            else:
                finish(qb, m, l, acc)
            return c

        lax.fori_loop(0, count, block, 0)

    qx.wait_recv()
    phase(lambda i: i, 4, [lambda qb: 2 * z + 1 - qb % 2], True, None)

    zb, za, zo = (z + 3) % 4, (z + 1) % 4, (z + 2) % 4

    def forward_up(t, c):
        slot = kv.at[2 * zb, t]
        wait_bytes(slot, up_recv.at[t])
        remote(slot, slot, up2_send, up2_recv, above).start()
        return c

    def forward_dn(t, c):
        slot = kv.at[2 * za + 1, t]
        wait_bytes(slot, dn_recv.at[8 + t])
        remote(slot, slot, dn2_send, dn2_recv, below).start()
        return c

    wait_bytes(kv.at[pl.ds(8, 2)], f_recv)
    phase(lambda i: i, 4, [lambda qb: 8 + qb % 2], False, None)

    lax.fori_loop(0, 8, forward_up, 0)
    lax.fori_loop(0, 8, forward_dn, 0)

    def rest_up(t, c):
        wait_bytes(kv.at[2 * zb + 1, t], up_recv.at[8 + t])
        wait_bytes(kv.at[2 * za, t], dn_recv.at[t])
        return c

    lax.fori_loop(0, 8, rest_up, 0)
    phase(lambda i: i, 4,
          [lambda qb: 2 * zb, lambda qb: 2 * za + 1, lambda qb: 2 * zb + 1, lambda qb: 2 * za], False, None)

    wait_bytes(kv.at[2 * zo], up2_recv)
    wait_bytes(kv.at[2 * zo + 1], dn2_recv)
    far = [lambda qb: 2 * zo, lambda qb: 2 * zo + 1]

    def hand_over(qb, m, l, acc):
        pb = qb % 2
        po[pb] = (acc / l).astype(BF16)
        pml[pb, 0:4] = jnp.broadcast_to(m, (4, QB))
        pml[pb, 4:8] = jnp.broadcast_to(l, (4, QB))
        remote(po.at[pb], po_in.at[pb], po_send.at[pb], po_recv.at[pb], partner).start()
        remote(pml.at[pb], pml_in.at[pb], pml_send.at[pb], pml_recv.at[pb], partner).start()

    def combine(qb, m, l, acc):
        pb = qb % 2
        wait_bytes(po_in.at[pb], po_recv.at[pb])
        wait_bytes(pml_in.at[pb], pml_recv.at[pb])
        m2, l2 = pml_in[pb, 0:1], pml_in[pb, 4:5]
        top = jnp.maximum(m, m2)
        mine, other = jnp.exp2(m - top), jnp.exp2(m2 - top) * l2
        total = l * mine + other
        both = (acc * mine + po_in[pb].astype(F32) * other) / total
        a_out[pb] = both.T.astype(BF16).reshape(8, BLK, BLK)

        def give(d, c):
            t = (j + d) % 8
            to = (2 * z + pb, xh * 8 + t)

            @pl.when(pb * 8 + t != me)
            def _():
                remote(a_out.at[pb, t], a_in.at[my_head], a_send, a_recv, to).start()

            @pl.when(pb * 8 + t == me)
            def _():
                pltpu.make_async_copy(a_out.at[pb, t], a_in.at[my_head], a_recv).start()

            return c

        lax.fori_loop(0, 8, give, 0)

    phase(lambda i: 2 + i, 2, far, False, hand_over)
    phase(lambda i: i, 2, far, False, combine)

    weight_copy.wait()
    wait_bytes(a_in, a_recv)
    rows = jnp.concatenate([a_in[h] for h in range(16)], axis=1)

    def project(n, c):
        cols = pl.ds(pl.multiple_of(n * 512, 512), 512)
        out[:, cols] = jnp.dot(rows, wbuf[:, cols], preferred_element_type=F32).astype(BF16)
        return c

    lax.fori_loop(0, 6, project, 0)

    wait_bytes(qbuf.at[0, 0], qx_send)
    wait_bytes(qbuf.at[0, 1], qx_send)
    wait_bytes(a_out.at[0], up2_send)
    wait_bytes(a_out.at[0], up2_send)
    wait_bytes(a_out.at[0], dn2_send)
    wait_bytes(a_out.at[0], dn2_send)
    wait_bytes(send_s, up_send)
    wait_bytes(send_s, dn_send)
    wait_bytes(a_in.at[pl.ds(0, 15)], q_send)
    wait_bytes(a_in.at[pl.ds(0, 15)], a_send)
    wait_bytes(send_s.at[pl.ds(0, 15)], s_send)
    wait_bytes(send_s.at[pl.ds(0, 15)], f_send)
    for pb in range(2):
        wait_bytes(po.at[pb], po_send.at[pb])
        wait_bytes(pml.at[pb], pml_send.at[pb])


def on_device(fresh_qkv, stale_kv, out_weight):
    fresh, stale = jnp.transpose(fresh_qkv, (1, 0, 2)), jnp.transpose(stale_kv, (1, 0, 2))
    vmem = pl.BlockSpec(memory_space=pltpu.VMEM)
    dma = pltpu.SemaphoreType.DMA
    rows, width = fresh.shape[1], out_weight.shape[1]
    return pl.pallas_call(
        kernel,
        out_shape=jax.ShapeDtypeStruct((rows, width), BF16),
        in_specs=[vmem, vmem, pl.BlockSpec(memory_space=pl.ANY)],
        out_specs=vmem,
        scratch_shapes=[
            pltpu.VMEM(out_weight.shape, BF16),
            pltpu.VMEM((16, 2, BLK, BLK), BF16),
            pltpu.VMEM((16, 2, BLK, BLK), BF16),
            pltpu.VMEM((10, 8, 2, BLK, BLK), BF16),
            pltpu.VMEM((2, 2, 8, BLK, BLK), BF16),
            pltpu.VMEM((4, BLK, QB), F32),
            pltpu.VMEM((4, 8, QB), F32),
            pltpu.VMEM((4, 8, QB), F32),
            pltpu.VMEM((STEP, QB), F32),
            pltpu.VMEM((2, BLK, QB), BF16),
            pltpu.VMEM((2, 8, QB), F32),
            pltpu.VMEM((2, BLK, QB), BF16),
            pltpu.VMEM((2, 8, QB), F32),
            pltpu.VMEM((2, 8, BLK, BLK), BF16),
            pltpu.VMEM((16, BLK, BLK), BF16),
            dma, dma, dma, dma, dma, dma, dma((16,)), dma, dma,
            dma, dma((16,)), dma, dma((16,)), dma, dma, dma, dma,
            dma((2,)), dma((2,)), dma((2,)), dma((2,)), dma, dma, dma,
        ],
        compiler_params=pltpu.CompilerParams(
            collective_id=0, has_side_effects=True, vmem_limit_bytes=60 * 2 ** 20),
        cost_estimate=pl.CostEstimate(flops=19 * 10 ** 9, bytes_accessed=16 * 2 ** 20, transcendentals=2 ** 25),
    )(fresh, stale, out_weight)


def solution(mesh):
    return jax.shard_map(
        on_device,
        mesh=mesh,
        in_specs=(P(("patch", "head"), None, None), P(("patch", "head"), None, None), P()),
        out_specs=P(("patch", "head"), None),
        check_vma=False,
    )
```

time: 444 us -> 109 us (0.25)
  the two profiles are of different devices: /device:TPU:1 before, /device:TPU:3 now
where the time goes in v1:
time: 109 us
  Pallas kernels  104 us (95%)
  local copies, waits for them, and re-layouts  4.63 us (4%)
    pallas_call x1, Pallas kernels, on_device(): pl.pallas_call(kernel, out_shape=jax.ShapeDtypeStruct((rows, width), BF16...  104 us
    unnamed x2, local copies, waits for them, and re-layouts  4.63 us

profile of v1, /device:TPU:3, one launch (start us, length us, event | category | flops | bytes accessed | tf_op | source)
XLA Modules:
  0.0 108.7 jit_solution(3109583800333100438)
XLA Ops:
  0.0 2.6 %copy.6 = bf16[128,2,2048]{2,0,1:T(8,128)(2,1)} copy(bf16[128,2,2048]{2,1,0:T(2,128)(2,1)} %param.4) | data formatting | bytes 2097152 | tf_op args[1]
  2.6 104.0 %shard_map.37 = bf16[128,3072]{1,0:T(8,128)(2,1)} custom-call(bf16[3,128,2048]{2,1,0:T(8,128)(2,1)} %bitcast.5, bf16[2,128,2048]{2,1,0:T(8,128)(2,1)} %bitcast.4, bf16[2048,3072]{1,0:T(8,128)(2,1)} %weight.1), custom_call_target="tpu_custom_call" | custom-call | flops 19000000512 | bytes 16777216 | tf_op jit(solution)/shard_map/pallas_call | solution.py:261
  106.6 2.1 %copy.8 = bf16[128,3072]{1,0:T(8,128)(2,1)} copy(bf16[128,3072]{1,0:T(8,128)(2,1)} %shard_map.37) | data formatting | bytes 1572864
